TPU v7x, 256 devices: a whole 4x4x8 slice. The times are simulated.
256 devices in a mesh: dp: 4 (over y), seq: 64 (over z, x, core).
Axes of the slice: x: 4, y: 4, z: 8, core: 2. Of those that a mesh axis runs over, the one named last changes fastest.
Arguments:
- qkv: bfloat16 [4, 12, 16384, 384], P('dp', None, 'seq'), may hold values from -12 to 12
- out_weight: bfloat16 [1536, 1536], P(('dp', 'seq')), may hold values from -0.5 to 0.5
- grad_projected: bfloat16 [4, 16384, 1536], P('dp', 'seq'), may hold values from -1.5 to 1.5
- group_span: int32 [4, 64], P('dp'), may hold values from 1 to 4, as said below
- clip_length: int32 [4, 64], P('dp'), may hold values from 16 to 1024, as said below
Outputs:
- projected: bfloat16 [4, 16384, 1536], P('dp', 'seq')
- grad_qkv: bfloat16 [4, 12, 16384, 384], P('dp', None, 'seq')
- grad_weight: float32 [1536, 1536], P(('dp', 'seq'))
Inputs may be any that keep to these rules, and one draw needn't show every extreme that they name: `group_span`: each entry is a power of two; along seq the devices of each row form aligned groups of that many consecutive devices, every device holding its group's size; the first 4 devices of every row form one group. `clip_length`: equal on all devices of a group; for a group of g devices it lies between (g - 1) * 256 + 16 and g * 256; the group of the first 4 devices of every row has length 1024.
All inputs are finite; a program needn't handle non-finite values.
Results may differ from a plain program's by a relative error of at most 0.012.
The roundings to bfloat16 on the way count: a program that leaves them out, or rounds other values in their place, can miss the bound.
Values may be sent and summed in bfloat16 or wider, within the bound.
A program may use at most 128 MiB of HBM per device.

v0:
```python
import math

import jax
import jax.numpy as jnp
from jax import lax
from jax.sharding import PartitionSpec as P

SECTIONS = 2


SCORE_FLOOR = -1e30


def swapped_2(block, axis, distance):
    count = lax.axis_size(axis)
    route = []
    for low in range(count):
        high = low | 1 << distance
        if high != low and high < count:
            route += [(low, high), (high, low)]
    return lax.ppermute(block, axis, route)


def lookup(table_row, position):
    marks = jnp.arange(table_row.shape[0], dtype=jnp.int32) == position
    return jnp.sum(jnp.where(marks, table_row, 0))


def butterfly(blocks, group_size, my_rank, transfer):
    slot_count = blocks.shape[0]
    for section_index in range(SECTIONS):
        stride = 1 << section_index
        shaped = blocks.reshape((slot_count // (2 * stride), 2, stride) + blocks.shape[1:])
        upper_half = my_rank >> section_index & 1 == 1
        outgoing = jnp.where(upper_half, shaped[:, 0], shaped[:, 1])
        incoming = transfer(outgoing, section_index)
        lower_part = jnp.where(upper_half, incoming, shaped[:, 0])
        upper_part = jnp.where(upper_half, shaped[:, 1], incoming)
        swapped = jnp.stack([lower_part, upper_part], axis=1)
        blocks = jnp.where(group_size > stride, swapped, shaped).reshape(blocks.shape)
    return blocks


def weight_gradient(attn_rows, grad_rows):
    return lax.psum_scatter(
        jnp.dot(attn_rows, grad_rows, preferred_element_type=jnp.float32),
        ("dp", "seq"),
        scatter_dimension=0,
        tiled=True,
    )


def local(qkv, out_weight, grad_projected, group_span, clip_length):
    my_rank = lax.axis_index("seq")
    group_size = lookup(group_span[0], my_rank)
    live_length = lookup(clip_length[0], my_rank)
    head_count = qkv.shape[1]
    tok_rows = qkv.shape[2]
    head_width = qkv.shape[3] // 3
    total_rows = head_count * tok_rows
    tile_rows = math.gcd(total_rows, 512)
    tile_count = total_rows // tile_rows
    score_scale = head_width ** (-0.5)
    weight_full = lax.all_gather(out_weight, ("dp", "seq"), axis=0, tiled=True)
    weight_cube = weight_full.reshape(head_count, head_width, weight_full.shape[1])
    packed = butterfly(
        qkv[0],
        group_size,
        my_rank,
        lambda half_block, section_bit: swapped_2(half_block, "seq", section_bit),
    )
    packed = packed.reshape(total_rows, 3 * head_width)
    head_rows = group_size * tok_rows
    row_ids = jnp.arange(total_rows, dtype=jnp.int32)
    row_head = row_ids // head_rows
    key_live = row_ids - row_head * head_rows < live_length

    def rows_of(array, row_start):
        return lax.dynamic_slice_in_dim(array, row_start, tile_rows)

    def partner_range(tile_index):
        first_row = tile_index * tile_rows
        last_row = first_row + tile_rows - 1
        low_row = first_row // head_rows * head_rows
        high_row = (last_row // head_rows + 1) * head_rows
        return (low_row // tile_rows, (high_row + tile_rows - 1) // tile_rows)

    def masked_scores(query_piece, query_start, key_start):
        key_piece = rows_of(packed, key_start)[:, head_width : 2 * head_width]
        raw_scores = (
            jnp.einsum("qd,kd->qk", query_piece, key_piece, preferred_element_type=jnp.float32)
            * score_scale
        )
        query_head = rows_of(row_head, query_start)
        key_head = rows_of(row_head, key_start)
        key_ok = rows_of(key_live, key_start)
        allowed = (query_head[:, None] == key_head[None, :]) & key_ok[None, :]
        return (raw_scores, allowed)

    def forward_tile(tile_index):
        query_start = tile_index * tile_rows
        query_piece = rows_of(packed, query_start)[:, :head_width]
        low_tile, high_tile = partner_range(tile_index)

        def stats_step(key_tile, carry):
            run_max, run_total = carry
            raw_scores, allowed = masked_scores(query_piece, query_start, key_tile * tile_rows)
            scores = jnp.where(allowed, raw_scores, SCORE_FLOOR)
            new_max = jnp.maximum(run_max, jnp.max(scores, axis=1))
            weights = jnp.where(allowed, jnp.exp(scores - new_max[:, None]), 0.0)
            run_total = run_total * jnp.exp(run_max - new_max) + jnp.sum(weights, axis=1)
            return (new_max, run_total)

        start_state = (
            jnp.full((tile_rows,), SCORE_FLOOR, jnp.float32),
            jnp.zeros((tile_rows,), jnp.float32),
        )
        run_max, run_total = lax.fori_loop(low_tile, high_tile, stats_step, start_state)
        log_total = run_max + jnp.log(run_total)

        def output_step(key_tile, accumulated):
            key_start = key_tile * tile_rows
            raw_scores, allowed = masked_scores(query_piece, query_start, key_start)
            probabilities = jnp.where(
                allowed, jnp.exp(raw_scores - log_total[:, None]), 0.0
            ).astype(jnp.bfloat16)
            value_piece = rows_of(packed, key_start)[:, 2 * head_width :]
            return accumulated + jnp.dot(
                probabilities, value_piece, preferred_element_type=jnp.float32
            )

        accumulated = lax.fori_loop(
            low_tile, high_tile, output_step, jnp.zeros((tile_rows, head_width), jnp.float32)
        )
        return (accumulated.astype(jnp.bfloat16), log_total)

    out_tiles, lse_tiles = lax.map(forward_tile, jnp.arange(tile_count, dtype=jnp.int32))
    out_all = out_tiles.reshape(total_rows, head_width)
    lse_all = lse_tiles.reshape(total_rows)
    attn_seq = butterfly(
        out_all.reshape(head_count, tok_rows, head_width),
        group_size,
        my_rank,
        lambda half_block, section_bit: swapped_2(half_block, "seq", section_bit),
    )
    grad_rows = grad_projected[0]
    projected = jnp.einsum(
        "htd,hde->te", attn_seq, weight_cube, preferred_element_type=jnp.float32
    ).astype(jnp.bfloat16)
    grad_attended = jnp.einsum(
        "te,hde->htd", grad_rows, weight_cube, preferred_element_type=jnp.float32
    ).astype(jnp.bfloat16)
    attn_rows = attn_seq.transpose(0, 2, 1).reshape(head_count * head_width, tok_rows)

    def attention_backward():
        grad_heads = butterfly(
            grad_attended,
            group_size,
            my_rank,
            lambda half_block, section_bit: swapped_2(half_block, "seq", section_bit),
        )
        grad_heads = grad_heads.reshape(total_rows, head_width)
        delta_all = jnp.sum(grad_heads.astype(jnp.float32) * out_all.astype(jnp.float32), axis=1)

        def backward_tile(query_total, key_tile):
            key_start = key_tile * tile_rows
            key_block = rows_of(packed, key_start)
            key_piece = key_block[:, head_width : 2 * head_width]
            value_piece = key_block[:, 2 * head_width :]
            low_tile, high_tile = partner_range(key_tile)

            def query_step(query_tile, carry):
                query_total, key_grad, value_grad = carry
                query_start = query_tile * tile_rows
                query_piece = rows_of(packed, query_start)[:, :head_width]
                grad_piece = rows_of(grad_heads, query_start)
                lse_piece = rows_of(lse_all, query_start)
                delta_piece = rows_of(delta_all, query_start)
                raw_scores, allowed = masked_scores(query_piece, query_start, key_start)
                probabilities = jnp.where(allowed, jnp.exp(raw_scores - lse_piece[:, None]), 0.0)
                prob_half = probabilities.astype(jnp.bfloat16)
                grad_probs = jnp.einsum(
                    "qd,kd->qk", grad_piece, value_piece, preferred_element_type=jnp.float32
                )
                grad_scores = (probabilities * (grad_probs - delta_piece[:, None])).astype(
                    jnp.bfloat16
                )
                value_grad = value_grad + jnp.einsum(
                    "qk,qd->kd", prob_half, grad_piece, preferred_element_type=jnp.float32
                )
                key_grad = key_grad + jnp.einsum(
                    "qk,qd->kd", grad_scores, query_piece, preferred_element_type=jnp.float32
                )
                query_term = jnp.dot(grad_scores, key_piece, preferred_element_type=jnp.float32)
                previous = rows_of(query_total, query_start)
                query_total = lax.dynamic_update_slice_in_dim(
                    query_total, previous + query_term, query_start, 0
                )
                return (query_total, key_grad, value_grad)

            zeros_tile = jnp.zeros((tile_rows, head_width), jnp.float32)
            query_total, key_grad, value_grad = lax.fori_loop(
                low_tile, high_tile, query_step, (query_total, zeros_tile, zeros_tile)
            )
            return (query_total, (key_grad, value_grad))

        query_grad, (key_tiles, value_tiles) = lax.scan(
            backward_tile,
            jnp.zeros((total_rows, head_width), jnp.float32),
            jnp.arange(tile_count, dtype=jnp.int32),
        )
        key_grad_all = key_tiles.reshape(total_rows, head_width)
        value_grad_all = value_tiles.reshape(total_rows, head_width)
        grad_packed = jnp.concatenate(
            [
                (query_grad * score_scale).astype(jnp.bfloat16),
                (key_grad_all * score_scale).astype(jnp.bfloat16),
                value_grad_all.astype(jnp.bfloat16),
            ],
            axis=1,
        )
        grad_packed = grad_packed.reshape(head_count, tok_rows, 3 * head_width)
        return butterfly(
            grad_packed,
            group_size,
            my_rank,
            lambda half_block, section_bit: swapped_2(half_block, "seq", section_bit),
        )

    grad_qkv = attention_backward()
    grad_weight = weight_gradient(attn_rows, grad_rows)
    return (projected[None], grad_qkv[None], grad_weight)


def solution(mesh):
    in_specs = (
        P("dp", None, "seq", None),
        P(("dp", "seq"), None),
        P("dp", "seq", None),
        P("dp", None),
        P("dp", None),
    )
    out_specs = (P("dp", "seq", None), P("dp", None, "seq", None), P(("dp", "seq"), None))
    return jax.shard_map(local, mesh=mesh, in_specs=in_specs, out_specs=out_specs, check_vma=False)
```

profile of v0, /device:TPU:1, one launch (start us, length us, event | category | flops | bytes accessed | tf_op | source)
XLA Modules:
  0.0 1641.4 jit_solution(17335635749640743493)
XLA Ops:
  23.1 26.0 %collective-permute-done.1 = bf16[3,2,256,384]{3,2,0,1:T(8,128)(2,1)} collective-permute-done((bf16[3,2,256,384]{3,2,0,1:T(8,128)(2,1)}, bf16[3,2,256,384]{3,2,0,1:T(8,128)(2,1)}, u32[]{:S(2)}, u32[]{:S(2)}) %collective-permute-start.1) | collective-permute-done | bytes 1179680 | tf_op jit(solution)/shard_map/ppermute | solution.py:21
  54.2 88.9 %while.145 = (s32[]{:T(128)}, bf16[6,512,128]{2,1,0:T(8,128)(2,1)}, f32[6,512]{1,0:T(8,128)}, s32[6]{0:T(128)}, s32[]{:T(128)}, /*index=5*/s32[]{:T(128)}, bf16[...) while((s32[]{:T(128)}, bf16[6,512,128]{2,1,0:T(8,128)(2,1)}, ...), condition=%wide.region_9.10_spmd.clone.clone, body=%wide.region_2.9_spmd.clone.clone.sunk | while | flops 205687360 | bytes 4284465 | solution.py:137
  75.0 6.8 while.148
  89.8 6.8 while.148
  104.7 6.8 while.148
  119.5 6.8 while.148
  134.3 6.8 while.148
  161.1 8.4 reshape.235
  204.1 101.8 %while.142 = (s32[]{:T(128)}, f32[3072,128]{1,0:T(8,128)S(1)}, f32[6,512,128]{2,1,0:T(8,128)}, bf16[6,512,128]{2,1,0:T(8,128)(2,1)}, s32[6]{0:T(128)}, /*index=5...) while((s32[]{:T(128)}, f32[3072,128]{1,0:T(8,128)S(1)}, ...), condition=%wide.region_14.15_spmd, body=%wide.region_11.14_spmd.sunk | while | flops 338100288 | bytes 10119946 | solution.py:207
  209.8 10.5 while.146
  226.8 10.5 while.146
  243.7 10.5 while.146
  260.7 10.5 while.146
  277.6 10.5 while.146
  294.5 10.5 while.146
  310.9 714.1 %fusion.2 = f32[8,1536]{1,0:T(8,128)S(1)} fusion(f32[1536,1536]{1,0:T(8,128)} %fusion.52), kind=kCustom, calls=%all-reduce-scatter | all-reduce-scatter fusion | flops 3145729 | bytes 9486336
  1046.0 22.1 %collective-permute-start.55 = (f32[8,1536]{1,0:T(8,128)S(1)}, f32[8,1536]{1,0:T(8,128)S(1)}, u32[]{:S(2)}, u32[]{:S(2)}) collective-permute-start(f32[8,1536]{1,0:T(8,128)S(1)} %fusion.2), channel_id=1, source_target_pairs={{0,48},{1,49},{2,50},{3,51},{4,52},{5,53},{6,54},{7,55},{8,56},{9,... | collective-permute-start | bytes 147464
  1123.1 7.9 collective-permute-start.38
  1138.1 13.1 collective-permute-start.36
  1151.3 13.3 collective-permute-start.35
  1164.6 13.1 collective-permute-start.34
  1177.8 13.1 collective-permute-start.33
  1190.9 13.1 collective-permute-start.32
  1206.9 12.9 collective-permute-start.31
  1219.8 13.1 collective-permute-start.30
  1232.9 13.1 collective-permute-start.29
  1246.1 13.1 collective-permute-start.28
  1259.2 13.1 collective-permute-start.27
  1272.4 13.1 collective-permute-start.26
  1285.5 13.1 collective-permute-start.25
  1298.7 13.1 collective-permute-start.24
  1311.8 13.1 collective-permute-start.23
  1325.0 13.1 collective-permute-start.22
  1338.1 13.1 collective-permute-start.21
  1351.3 13.1 collective-permute-start.20
  1364.4 13.1 collective-permute-start.19
  1377.6 13.1 collective-permute-start.18
  1390.7 13.1 collective-permute-start.17
  1403.9 13.1 collective-permute-start.16
  1417.0 13.1 collective-permute-start.15
  1430.2 13.1 collective-permute-start.14
  1443.3 13.1 collective-permute-start.13
  1456.5 13.1 collective-permute-start.12
  1469.6 13.8 collective-permute-start.11
  1483.4 13.1 collective-permute-start.10
  1496.5 13.1 collective-permute-start.9
  1509.7 12.5 collective-permute-start.8
  1525.1 97.3 %concatenate.18 = f32[518,1536]{1,0:T(8,128)} concatenate(f32[6,1536]{1,0:T(8,128)S(1)} %collective-permute-done.71, f32[8,1536]{1,0:T(8,128)S(1)} %collective-permute-done.70, f32[8,1536]{1,0:T(8,128)S(1)} %collective-permute-done.69, f32[8,1536]{1,0:T(8,128)S(1)} %collective-permute-done.68, f32[8,1536]{1,0:T(8,128)S(1)} %collective-permute-done.67, ...), dimensions={0} | concatenate | bytes 6365184
  (693 shorter events, 374.0 us)
Async XLA Ops:
  7.2 153.9 %all-gather.3.cloned.1.call-start = ((), (), s32[]{:S(2)}) async-start(), calls=%async_computation | async-start | bytes 6316032 | tf_op jit(solution)/shard_map/all_gather | solution.py:64
  21.5 27.7 %collective-permute-start.1 = (bf16[3,2,256,384]{3,2,0,1:T(8,128)(2,1)}, bf16[3,2,256,384]{3,2,0,1:T(8,128)(2,1)}, u32[]{:S(2)}, u32[]{:S(2)}) collective-permute-start(bf16[3,2,256,384]{3,2,0,1:T(8,128)(2,1)} %broadcast_select_fusion.7), channel_id=1, source_target_pairs={{0,2},{2,0},{1,3},{3,1},{4,6},{6,4},{5,7},{7,5},{8,10},{10,8},{9,1... | collective-permute-start | bytes 3538952 | tf_op jit(solution)/shard_map/ppermute | solution.py:21
  310.1 797.9 %collective-permute-start.6 = (bf16[6,1,256,384]{3,2,0,1:T(8,128)(2,1)}, bf16[6,1,256,384]{3,2,0,1:T(8,128)(2,1)}, u32[]{:S(2)}, u32[]{:S(2)}) collective-permute-start(bf16[6,1,256,384]{3,2,0,1:T(8,128)(2,1)} %broadcast_select_fusion.2), channel_id=1, source_target_pairs={{0,1},{1,0},{2,3},{3,2},{4,5},{5,4},{6,7},{7,6},{8,9},{9,8},{10,11... | collective-permute-start | bytes 3538952 | tf_op jit(solution)/shard_map/ppermute | solution.py:21
  1042.1 26.1 %collective-permute-start.58 = (f32[8,1536]{1,0:T(8,128)S(1)}, f32[8,1536]{1,0:T(8,128)S(1)}, u32[]{:S(2)}, u32[]{:S(2)}) collective-permute-start(f32[8,1536]{1,0:T(8,128)S(1)} %fusion.2), channel_id=1, source_target_pairs={{0,51},{1,52},{2,53},{3,54},{4,55},{5,56},{6,57},{7,58},{8,59},{9,... | collective-permute-start | bytes 147464
  1043.4 27.3 %collective-permute-start.57 = (f32[8,1536]{1,0:T(8,128)S(1)}, f32[8,1536]{1,0:T(8,128)S(1)}, u32[]{:S(2)}, u32[]{:S(2)}) collective-permute-start(f32[8,1536]{1,0:T(8,128)S(1)} %fusion.2), channel_id=1, source_target_pairs={{0,50},{1,51},{2,52},{3,53},{4,54},{5,55},{6,56},{7,57},{8,58},{9,... | collective-permute-start | bytes 147464
  1044.7 30.6 %collective-permute-start.56 = (f32[8,1536]{1,0:T(8,128)S(1)}, f32[8,1536]{1,0:T(8,128)S(1)}, u32[]{:S(2)}, u32[]{:S(2)}) collective-permute-start(f32[8,1536]{1,0:T(8,128)S(1)} %fusion.2), channel_id=1, source_target_pairs={{0,49},{1,50},{2,51},{3,52},{4,53},{5,54},{6,55},{7,56},{8,57},{9,... | collective-permute-start | bytes 147464
  1046.0 31.5 %collective-permute-start.55 = (f32[8,1536]{1,0:T(8,128)S(1)}, f32[8,1536]{1,0:T(8,128)S(1)}, u32[]{:S(2)}, u32[]{:S(2)}) collective-permute-start(f32[8,1536]{1,0:T(8,128)S(1)} %fusion.2), channel_id=1, source_target_pairs={{0,48},{1,49},{2,50},{3,51},{4,52},{5,53},{6,54},{7,55},{8,56},{9,... | collective-permute-start | bytes 147464
  1089.4 15.2 collective-permute-start.47
  1090.7 25.6 %collective-permute-start.46 = (f32[8,1536]{1,0:T(8,128)S(1)}, f32[8,1536]{1,0:T(8,128)S(1)}, u32[]{:S(2)}, u32[]{:S(2)}) collective-permute-start(f32[8,1536]{1,0:T(8,128)S(1)} %fusion.2), channel_id=1, source_target_pairs={{0,39},{1,40},{2,41},{3,42},{4,43},{5,44},{6,45},{7,46},{8,47},{9,... | collective-permute-start | bytes 147464
  1095.7 22.2 %collective-permute-start.45 = (f32[8,1536]{1,0:T(8,128)S(1)}, f32[8,1536]{1,0:T(8,128)S(1)}, u32[]{:S(2)}, u32[]{:S(2)}) collective-permute-start(f32[8,1536]{1,0:T(8,128)S(1)} %fusion.2), channel_id=1, source_target_pairs={{0,38},{1,39},{2,40},{3,41},{4,42},{5,43},{6,44},{7,45},{8,46},{9,... | collective-permute-start | bytes 147464
  1099.7 21.2 %collective-permute-start.44 = (f32[8,1536]{1,0:T(8,128)S(1)}, f32[8,1536]{1,0:T(8,128)S(1)}, u32[]{:S(2)}, u32[]{:S(2)}) collective-permute-start(f32[8,1536]{1,0:T(8,128)S(1)} %fusion.2), channel_id=1, source_target_pairs={{0,37},{1,38},{2,39},{3,40},{4,41},{5,42},{6,43},{7,44},{8,45},{9,... | collective-permute-start | bytes 147464
  1104.6 18.5 %collective-permute-start.43 = (f32[8,1536]{1,0:T(8,128)S(1)}, f32[8,1536]{1,0:T(8,128)S(1)}, u32[]{:S(2)}, u32[]{:S(2)}) collective-permute-start(f32[8,1536]{1,0:T(8,128)S(1)} %fusion.2), channel_id=1, source_target_pairs={{0,36},{1,37},{2,38},{3,39},{4,40},{5,41},{6,42},{7,43},{8,44},{9,... | collective-permute-start | bytes 147464
  1108.0 23.0 %collective-permute-start.42 = (f32[8,1536]{1,0:T(8,128)S(1)}, f32[8,1536]{1,0:T(8,128)S(1)}, u32[]{:S(2)}, u32[]{:S(2)}) collective-permute-start(f32[8,1536]{1,0:T(8,128)S(1)} %fusion.2), channel_id=1, source_target_pairs={{0,35},{1,36},{2,37},{3,38},{4,39},{5,40},{6,41},{7,42},{8,43},{9,... | collective-permute-start | bytes 147464
  1116.3 21.8 %collective-permute-start.41 = (f32[8,1536]{1,0:T(8,128)S(1)}, f32[8,1536]{1,0:T(8,128)S(1)}, u32[]{:S(2)}, u32[]{:S(2)}) collective-permute-start(f32[8,1536]{1,0:T(8,128)S(1)} %fusion.2), channel_id=1, source_target_pairs={{0,34},{1,35},{2,36},{3,37},{4,38},{5,39},{6,40},{7,41},{8,42},{9,... | collective-permute-start | bytes 147464
  1117.9 33.3 %collective-permute-start.40 = (f32[8,1536]{1,0:T(8,128)S(1)}, f32[8,1536]{1,0:T(8,128)S(1)}, u32[]{:S(2)}, u32[]{:S(2)}) collective-permute-start(f32[8,1536]{1,0:T(8,128)S(1)} %fusion.2), channel_id=1, source_target_pairs={{0,33},{1,34},{2,35},{3,36},{4,37},{5,38},{6,39},{7,40},{8,41},{9,... | collective-permute-start | bytes 147464
  1120.9 43.8 %collective-permute-start.39 = (f32[8,1536]{1,0:T(8,128)S(1)}, f32[8,1536]{1,0:T(8,128)S(1)}, u32[]{:S(2)}, u32[]{:S(2)}) collective-permute-start(f32[8,1536]{1,0:T(8,128)S(1)} %fusion.2), channel_id=1, source_target_pairs={{0,32},{1,33},{2,34},{3,35},{4,36},{5,37},{6,38},{7,39},{8,40},{9,... | collective-permute-start | bytes 147464
  1123.1 54.6 %collective-permute-start.38 = (f32[8,1536]{1,0:T(8,128)S(1)}, f32[8,1536]{1,0:T(8,128)S(1)}, u32[]{:S(2)}, u32[]{:S(2)}) collective-permute-start(f32[8,1536]{1,0:T(8,128)S(1)} %fusion.2), channel_id=1, source_target_pairs={{0,31},{1,32},{2,33},{3,34},{4,35},{5,36},{6,37},{7,38},{8,39},{9,... | collective-permute-start | bytes 147464
  1131.0 59.9 %collective-permute-start.37 = (f32[8,1536]{1,0:T(8,128)S(1)}, f32[8,1536]{1,0:T(8,128)S(1)}, u32[]{:S(2)}, u32[]{:S(2)}) collective-permute-start(f32[8,1536]{1,0:T(8,128)S(1)} %fusion.2), channel_id=1, source_target_pairs={{0,30},{1,31},{2,32},{3,33},{4,34},{5,35},{6,36},{7,37},{8,38},{9,... | collective-permute-start | bytes 147464
  1138.1 67.2 %collective-permute-start.36 = (f32[8,1536]{1,0:T(8,128)S(1)}, f32[8,1536]{1,0:T(8,128)S(1)}, u32[]{:S(2)}, u32[]{:S(2)}) collective-permute-start(f32[8,1536]{1,0:T(8,128)S(1)} %fusion.2), channel_id=1, source_target_pairs={{0,29},{1,30},{2,31},{3,32},{4,33},{5,34},{6,35},{7,36},{8,37},{9,... | collective-permute-start | bytes 147464
  1151.3 55.6 %collective-permute-start.35 = (f32[8,1536]{1,0:T(8,128)S(1)}, f32[8,1536]{1,0:T(8,128)S(1)}, u32[]{:S(2)}, u32[]{:S(2)}) collective-permute-start(f32[8,1536]{1,0:T(8,128)S(1)} %fusion.2), channel_id=1, source_target_pairs={{0,28},{1,29},{2,30},{3,31},{4,32},{5,33},{6,34},{7,35},{8,36},{9,... | collective-permute-start | bytes 147464
  1164.6 55.1 %collective-permute-start.34 = (f32[8,1536]{1,0:T(8,128)S(1)}, f32[8,1536]{1,0:T(8,128)S(1)}, u32[]{:S(2)}, u32[]{:S(2)}) collective-permute-start(f32[8,1536]{1,0:T(8,128)S(1)} %fusion.2), channel_id=1, source_target_pairs={{0,27},{1,28},{2,29},{3,30},{4,31},{5,32},{6,33},{7,34},{8,35},{9,... | collective-permute-start | bytes 147464
  1177.8 55.1 %collective-permute-start.33 = (f32[8,1536]{1,0:T(8,128)S(1)}, f32[8,1536]{1,0:T(8,128)S(1)}, u32[]{:S(2)}, u32[]{:S(2)}) collective-permute-start(f32[8,1536]{1,0:T(8,128)S(1)} %fusion.2), channel_id=1, source_target_pairs={{0,26},{1,27},{2,28},{3,29},{4,30},{5,31},{6,32},{7,33},{8,34},{9,... | collective-permute-start | bytes 147464
  1190.9 55.1 %collective-permute-start.32 = (f32[8,1536]{1,0:T(8,128)S(1)}, f32[8,1536]{1,0:T(8,128)S(1)}, u32[]{:S(2)}, u32[]{:S(2)}) collective-permute-start(f32[8,1536]{1,0:T(8,128)S(1)} %fusion.2), channel_id=1, source_target_pairs={{0,25},{1,26},{2,27},{3,28},{4,29},{5,30},{6,31},{7,32},{8,33},{9,... | collective-permute-start | bytes 147464
  1205.4 423.8 %collective-permute-start.7 = (bf16[3,2,256,384]{3,2,0,1:T(8,128)(2,1)}, bf16[3,2,256,384]{3,2,0,1:T(8,128)(2,1)}, u32[]{:S(2)}, u32[]{:S(2)}) collective-permute-start(bf16[3,2,256,384]{3,2,0,1:T(8,128)(2,1)} %broadcast_select_fusion.6), channel_id=1, source_target_pairs={{0,2},{2,0},{1,3},{3,1},{4,6},{6,4},{5,7},{7,5},{8,10},{10,8},{9,1... | collective-permute-start | bytes 3538952 | tf_op jit(solution)/shard_map/ppermute | solution.py:21
  1206.9 52.4 %collective-permute-start.31 = (f32[8,1536]{1,0:T(8,128)S(1)}, f32[8,1536]{1,0:T(8,128)S(1)}, u32[]{:S(2)}, u32[]{:S(2)}) collective-permute-start(f32[8,1536]{1,0:T(8,128)S(1)} %fusion.2), channel_id=1, source_target_pairs={{0,24},{1,25},{2,26},{3,27},{4,28},{5,29},{6,30},{7,31},{8,32},{9,... | collective-permute-start | bytes 147464
  1219.8 52.6 %collective-permute-start.30 = (f32[8,1536]{1,0:T(8,128)S(1)}, f32[8,1536]{1,0:T(8,128)S(1)}, u32[]{:S(2)}, u32[]{:S(2)}) collective-permute-start(f32[8,1536]{1,0:T(8,128)S(1)} %fusion.2), channel_id=1, source_target_pairs={{0,23},{1,24},{2,25},{3,26},{4,27},{5,28},{6,29},{7,30},{8,31},{9,... | collective-permute-start | bytes 147464
  1232.9 52.6 %collective-permute-start.29 = (f32[8,1536]{1,0:T(8,128)S(1)}, f32[8,1536]{1,0:T(8,128)S(1)}, u32[]{:S(2)}, u32[]{:S(2)}) collective-permute-start(f32[8,1536]{1,0:T(8,128)S(1)} %fusion.2), channel_id=1, source_target_pairs={{0,22},{1,23},{2,24},{3,25},{4,26},{5,27},{6,28},{7,29},{8,30},{9,... | collective-permute-start | bytes 147464
  1246.1 52.6 %collective-permute-start.28 = (f32[8,1536]{1,0:T(8,128)S(1)}, f32[8,1536]{1,0:T(8,128)S(1)}, u32[]{:S(2)}, u32[]{:S(2)}) collective-permute-start(f32[8,1536]{1,0:T(8,128)S(1)} %fusion.2), channel_id=1, source_target_pairs={{0,21},{1,22},{2,23},{3,24},{4,25},{5,26},{6,27},{7,28},{8,29},{9,... | collective-permute-start | bytes 147464
  1259.2 52.6 %collective-permute-start.27 = (f32[8,1536]{1,0:T(8,128)S(1)}, f32[8,1536]{1,0:T(8,128)S(1)}, u32[]{:S(2)}, u32[]{:S(2)}) collective-permute-start(f32[8,1536]{1,0:T(8,128)S(1)} %fusion.2), channel_id=1, source_target_pairs={{0,20},{1,21},{2,22},{3,23},{4,24},{5,25},{6,26},{7,27},{8,28},{9,... | collective-permute-start | bytes 147464
  1272.4 52.6 %collective-permute-start.26 = (f32[8,1536]{1,0:T(8,128)S(1)}, f32[8,1536]{1,0:T(8,128)S(1)}, u32[]{:S(2)}, u32[]{:S(2)}) collective-permute-start(f32[8,1536]{1,0:T(8,128)S(1)} %fusion.2), channel_id=1, source_target_pairs={{0,19},{1,20},{2,21},{3,22},{4,23},{5,24},{6,25},{7,26},{8,27},{9,... | collective-permute-start | bytes 147464
  1285.5 52.6 %collective-permute-start.25 = (f32[8,1536]{1,0:T(8,128)S(1)}, f32[8,1536]{1,0:T(8,128)S(1)}, u32[]{:S(2)}, u32[]{:S(2)}) collective-permute-start(f32[8,1536]{1,0:T(8,128)S(1)} %fusion.2), channel_id=1, source_target_pairs={{0,18},{1,19},{2,20},{3,21},{4,22},{5,23},{6,24},{7,25},{8,26},{9,... | collective-permute-start | bytes 147464
  1298.7 52.6 %collective-permute-start.24 = (f32[8,1536]{1,0:T(8,128)S(1)}, f32[8,1536]{1,0:T(8,128)S(1)}, u32[]{:S(2)}, u32[]{:S(2)}) collective-permute-start(f32[8,1536]{1,0:T(8,128)S(1)} %fusion.2), channel_id=1, source_target_pairs={{0,17},{1,18},{2,19},{3,20},{4,21},{5,22},{6,23},{7,24},{8,25},{9,... | collective-permute-start | bytes 147464
  1311.8 52.6 %collective-permute-start.23 = (f32[8,1536]{1,0:T(8,128)S(1)}, f32[8,1536]{1,0:T(8,128)S(1)}, u32[]{:S(2)}, u32[]{:S(2)}) collective-permute-start(f32[8,1536]{1,0:T(8,128)S(1)} %fusion.2), channel_id=1, source_target_pairs={{0,16},{1,17},{2,18},{3,19},{4,20},{5,21},{6,22},{7,23},{8,24},{9,... | collective-permute-start | bytes 147464
  1325.0 52.6 %collective-permute-start.22 = (f32[8,1536]{1,0:T(8,128)S(1)}, f32[8,1536]{1,0:T(8,128)S(1)}, u32[]{:S(2)}, u32[]{:S(2)}) collective-permute-start(f32[8,1536]{1,0:T(8,128)S(1)} %fusion.2), channel_id=1, source_target_pairs={{0,15},{1,16},{2,17},{3,18},{4,19},{5,20},{6,21},{7,22},{8,23},{9,... | collective-permute-start | bytes 147464
  1338.1 52.6 %collective-permute-start.21 = (f32[8,1536]{1,0:T(8,128)S(1)}, f32[8,1536]{1,0:T(8,128)S(1)}, u32[]{:S(2)}, u32[]{:S(2)}) collective-permute-start(f32[8,1536]{1,0:T(8,128)S(1)} %fusion.2), channel_id=1, source_target_pairs={{0,14},{1,15},{2,16},{3,17},{4,18},{5,19},{6,20},{7,21},{8,22},{9,... | collective-permute-start | bytes 147464
  1351.3 52.6 %collective-permute-start.20 = (f32[8,1536]{1,0:T(8,128)S(1)}, f32[8,1536]{1,0:T(8,128)S(1)}, u32[]{:S(2)}, u32[]{:S(2)}) collective-permute-start(f32[8,1536]{1,0:T(8,128)S(1)} %fusion.2), channel_id=1, source_target_pairs={{0,13},{1,14},{2,15},{3,16},{4,17},{5,18},{6,19},{7,20},{8,21},{9,... | collective-permute-start | bytes 147464
  1364.4 52.6 %collective-permute-start.19 = (f32[8,1536]{1,0:T(8,128)S(1)}, f32[8,1536]{1,0:T(8,128)S(1)}, u32[]{:S(2)}, u32[]{:S(2)}) collective-permute-start(f32[8,1536]{1,0:T(8,128)S(1)} %fusion.2), channel_id=1, source_target_pairs={{0,12},{1,13},{2,14},{3,15},{4,16},{5,17},{6,18},{7,19},{8,20},{9,... | collective-permute-start | bytes 147464
  1377.6 52.6 %collective-permute-start.18 = (f32[8,1536]{1,0:T(8,128)S(1)}, f32[8,1536]{1,0:T(8,128)S(1)}, u32[]{:S(2)}, u32[]{:S(2)}) collective-permute-start(f32[8,1536]{1,0:T(8,128)S(1)} %fusion.2), channel_id=1, source_target_pairs={{0,11},{1,12},{2,13},{3,14},{4,15},{5,16},{6,17},{7,18},{8,19},{9,... | collective-permute-start | bytes 147464
  1390.7 52.6 %collective-permute-start.17 = (f32[8,1536]{1,0:T(8,128)S(1)}, f32[8,1536]{1,0:T(8,128)S(1)}, u32[]{:S(2)}, u32[]{:S(2)}) collective-permute-start(f32[8,1536]{1,0:T(8,128)S(1)} %fusion.2), channel_id=1, source_target_pairs={{0,10},{1,11},{2,12},{3,13},{4,14},{5,15},{6,16},{7,17},{8,18},{9,... | collective-permute-start | bytes 147464
  1403.9 52.6 %collective-permute-start.16 = (f32[8,1536]{1,0:T(8,128)S(1)}, f32[8,1536]{1,0:T(8,128)S(1)}, u32[]{:S(2)}, u32[]{:S(2)}) collective-permute-start(f32[8,1536]{1,0:T(8,128)S(1)} %fusion.2), channel_id=1, source_target_pairs={{0,9},{1,10},{2,11},{3,12},{4,13},{5,14},{6,15},{7,16},{8,17},{9,1... | collective-permute-start | bytes 147464
  1417.0 52.6 %collective-permute-start.15 = (f32[8,1536]{1,0:T(8,128)S(1)}, f32[8,1536]{1,0:T(8,128)S(1)}, u32[]{:S(2)}, u32[]{:S(2)}) collective-permute-start(f32[8,1536]{1,0:T(8,128)S(1)} %fusion.2), channel_id=1, source_target_pairs={{0,8},{1,9},{2,10},{3,11},{4,12},{5,13},{6,14},{7,15},{8,16},{9,17... | collective-permute-start | bytes 147464
  1430.2 53.2 %collective-permute-start.14 = (f32[8,1536]{1,0:T(8,128)S(1)}, f32[8,1536]{1,0:T(8,128)S(1)}, u32[]{:S(2)}, u32[]{:S(2)}) collective-permute-start(f32[8,1536]{1,0:T(8,128)S(1)} %fusion.2), channel_id=1, source_target_pairs={{0,7},{1,8},{2,9},{3,10},{4,11},{5,12},{6,13},{7,14},{8,15},{9,16}... | collective-permute-start | bytes 147464
  1443.3 53.2 %collective-permute-start.13 = (f32[8,1536]{1,0:T(8,128)S(1)}, f32[8,1536]{1,0:T(8,128)S(1)}, u32[]{:S(2)}, u32[]{:S(2)}) collective-permute-start(f32[8,1536]{1,0:T(8,128)S(1)} %fusion.2), channel_id=1, source_target_pairs={{0,6},{1,7},{2,8},{3,9},{4,10},{5,11},{6,12},{7,13},{8,14},{9,15},... | collective-permute-start | bytes 147464
  1456.5 53.2 %collective-permute-start.12 = (f32[8,1536]{1,0:T(8,128)S(1)}, f32[8,1536]{1,0:T(8,128)S(1)}, u32[]{:S(2)}, u32[]{:S(2)}) collective-permute-start(f32[8,1536]{1,0:T(8,128)S(1)} %fusion.2), channel_id=1, source_target_pairs={{0,5},{1,6},{2,7},{3,8},{4,9},{5,10},{6,11},{7,12},{8,13},{9,14},{... | collective-permute-start | bytes 147464
  1469.6 52.9 %collective-permute-start.11 = (f32[8,1536]{1,0:T(8,128)S(1)}, f32[8,1536]{1,0:T(8,128)}, u32[]{:S(2)}, u32[]{:S(2)}) collective-permute-start(f32[8,1536]{1,0:T(8,128)S(1)} %fusion.2), channel_id=1, source_target_pairs={{0,4},{1,5},{2,6},{3,7},{4,8},{5,9},{6,10},{7,11},{8,12},{9,13},{1... | collective-permute-start | bytes 147464
  1483.4 39.1 %collective-permute-start.10 = (f32[8,1536]{1,0:T(8,128)S(1)}, f32[8,1536]{1,0:T(8,128)}, u32[]{:S(2)}, u32[]{:S(2)}) collective-permute-start(f32[8,1536]{1,0:T(8,128)S(1)} %fusion.2), channel_id=1, source_target_pairs={{0,3},{1,4},{2,5},{3,6},{4,7},{5,8},{6,9},{7,10},{8,11},{9,12},{10... | collective-permute-start | bytes 147464
  1496.5 26.0 %collective-permute-start.9 = (f32[8,1536]{1,0:T(8,128)S(1)}, f32[8,1536]{1,0:T(8,128)}, u32[]{:S(2)}, u32[]{:S(2)}) collective-permute-start(f32[8,1536]{1,0:T(8,128)S(1)} %fusion.2), channel_id=1, source_target_pairs={{0,2},{1,3},{2,4},{3,5},{4,6},{5,7},{6,8},{7,9},{8,10},{9,11},{10,... | collective-permute-start | bytes 147464
  1509.7 15.4 collective-permute-start.8
  (115 other events, 6029.8 us)
Sparse Core Ops, SparseCore 0:
  21.6 118.7 all-gather.2
where the time goes:
time: 1660 us; the launch traced here: 1640 us
  blocking collectives  714 us (43%)
  starting transfers between devices  499 us (30%)
  local copies, waits for them, and re-layouts  225 us (14%)
  matrix products  78.9 us (5%)
  other arithmetic  55 us (3%)
  waiting for transfers between devices  39.6 us (2%)
  between operations  18 us (1%)
    unnamed x1, blocking collectives  714 us
    unnamed x64, starting transfers between devices  490 us
    unnamed x173, local copies, waits for them, and re-layouts  105 us
    dynamic_slice x108, local copies, waits for them, and re-layouts, rows_of(): return lax.dynamic_slice_in_dim(array, row_start, tile_rows)  59.2 us
    ppermute x8, waiting for transfers between devices, swapped_2(): return lax.ppermute(block, axis, route)  36.8 us
  transfers between devices with their start and end apart: 73, of which 6 were waited for; matrix products, arithmetic and copies ran while one was open for 57% of the time, Pallas kernels for 0%

commit v1 on v0

v1 whole, which is shorter than its diff:
```python
import functools

import jax
import jax.numpy as jnp
from jax import lax
from jax.experimental import pallas as pl
from jax.experimental.pallas import tpu as pltpu
from jax.sharding import PartitionSpec as P

HEADS = 12
DIM = 128
TOK = 256
WIDTH = 1536
HALF = WIDTH // 2
NY = 4
NZ = 8
NX = 4
SLAB = 48
BLOCK = SLAB * NZ
OWN_HEADS = HEADS // NY
CHIP_ROWS = 12
DEV_ROWS = 6
AHEAD = 4
FLOOR = -1e30
SCALE = DIM**-0.5
LOG2E = 1.4426950408889634
MESH = pl.DeviceIdType.MESH
F32 = jnp.float32
BF16 = jnp.bfloat16


def mm(a, b, dims):
    return lax.dot_general(a, b, (dims, ((), ())), preferred_element_type=F32)


NN = ((1,), (0,))
NT = ((1,), (1,))
TN = ((0,), (0,))


def kernel(
    qkv, w_own, gp, span, clip,
    proj_o, grad_o, gw_o,
    q_s, kv, bias_s, w_all, o_s, lse_s,
    w_send, w_pair, w_tmp, w_x, w_slab,
    g_tmp, g_acc, g_send, g_recv, gy_send, gy_recv, gz_send, gz_recv,
    gx_in, gx_send, gx_recv, gc_send, gc_recv,
    d_own, d_rs, d_sib, d_sib_r, d_x, d_x_r,
    loc_sem, ks_s, ks_r, kx_s, kx_r, kf_s, kf_r,
    wa_s, wa_r, wx_s, wx_r, wz_s, wz_r, wy_s, wy_r, wf_s, wf_r, wb_s, wb_r,
    gs_s, gs_r, gy_s, gy_r, gz_s, gz_r, gx_s, gx_r, gc_s, gc_r,
    ds_s, ds_r, dx_s, dx_r,
):
    me = lax.axis_index("seq")
    y = lax.axis_index("dp")
    c = me % 2
    x = (me // 2) % NX
    z = me // (2 * NX)
    sib = me + 1 - 2 * c
    far = me + 2 - 4 * (x % 2)
    cross = far + 1 - 2 * c

    def at_x(xx):
        return {"seq": (z * NX + xx) * 2 + c}

    def at_z(zz):
        return {"seq": (zz * NX + x) * 2 + c}

    def at_y(yy):
        return {"dp": yy}

    at_sib = {"seq": sib}
    at_far = {"seq": far}

    def rdma(src, dst, send, recv, device):
        return pltpu.make_async_remote_copy(
            src_ref=src, dst_ref=dst, send_sem=send, recv_sem=recv,
            device_id=device, device_id_type=MESH,
        )

    partners = [at_sib]
    partners += [at_x((x + d) % NX) for d in range(1, NX)]
    partners += [at_z((z + d) % NZ) for d in range(1, NZ)]
    partners += [at_y((y + d) % NY) for d in range(1, NY)]
    barrier = pltpu.get_barrier_semaphore()
    for partner in partners:
        pl.semaphore_signal(barrier, inc=1, device_id=partner, device_id_type=MESH)
    pl.semaphore_wait(barrier, len(partners))

    def head(i):
        return (OWN_HEADS * (y + 1) + i) % HEADS

    def kv_sib(i):
        return rdma(qkv.at[0, head(i), :, pl.ds(DIM, 2 * DIM)], kv.at[i, 1], ks_s.at[i], ks_r.at[i], at_sib)

    def kv_far(i):
        return rdma(qkv.at[0, head(i), :, pl.ds(DIM, 2 * DIM)], kv.at[i, 2], kx_s.at[i], kx_r.at[i], at_far)

    def kv_relay(i):
        return rdma(kv.at[i, 2], kv.at[i, 3], kf_s.at[i], kf_r.at[i], at_sib)

    def kv_own(i):
        return pltpu.make_async_copy(qkv.at[0, head(i), :, pl.ds(DIM, 2 * DIM)], kv.at[i, 0], loc_sem.at[1 + i])

    q_copy = pltpu.make_async_copy(qkv.at[0, :, :, pl.ds(0, DIM)], q_s, loc_sem.at[0])

    mine = pl.ds(pl.multiple_of(c * HALF, HALF), HALF)
    other = pl.ds(pl.multiple_of((1 - c) * HALF, HALF), HALF)

    def slab(yy, zz):
        return w_all.at[pl.ds(pl.multiple_of(SLAB * (NZ * yy + zz), 16), SLAB), mine]

    pair_copy = rdma(w_send, w_pair.at[c], wa_s, wa_r, at_sib)
    pair_wait = rdma(w_send, w_pair.at[1 - c], wa_s, wa_r, at_sib)

    def x_copy(d):
        return rdma(w_x.at[x], w_x.at[x], wx_s.at[d - 1], wx_r.at[d - 1], at_x((x + d) % NX))

    def x_wait(d):
        back = (x + NX - d) % NX
        return rdma(w_x.at[back], w_x.at[back], wx_s.at[d - 1], wx_r.at[d - 1], at_x(back))

    def z_copy(d):
        return rdma(slab(y, z), slab(y, z), wz_s.at[d - 1], wz_r.at[d - 1], at_z((z + d) % NZ))

    def z_wait(d):
        back = (z + NZ - d) % NZ
        return rdma(slab(y, back), slab(y, back), wz_s.at[d - 1], wz_r.at[d - 1], at_z(back))

    up, down = (y + 1) % NY, (y + NY - 1) % NY
    opposite = (y + 2) % NY

    def y_copy(d, way):
        zz = (z + NZ - d) % NZ
        return rdma(slab(y, zz), slab(y, zz), wy_s.at[d, way], wy_r.at[d, way], at_y(up if way == 0 else down))

    def y_wait(d, way):
        zz = (z + NZ - d) % NZ
        yy = down if way == 0 else up
        return rdma(slab(yy, zz), slab(yy, zz), wy_s.at[d, way], wy_r.at[d, way], at_y(yy))

    def y_relay(d):
        zz = (z + NZ - d) % NZ
        odd = d % 2
        yy = (y + NY - 1 + 2 * odd) % NY
        to = (y + 1 + 2 * odd) % NY
        return rdma(slab(yy, zz), slab(yy, zz), wf_s.at[d], wf_r.at[d], at_y(to))

    def y_relay_wait(d):
        zz = (z + NZ - d) % NZ
        return rdma(slab(opposite, zz), slab(opposite, zz), wf_s.at[d], wf_r.at[d], at_y(up))

    def rows_block(yy, columns):
        return w_all.at[pl.ds(pl.multiple_of(BLOCK * yy, 16), BLOCK), columns]

    def block_copy(k):
        yy = (y, down, up, opposite)[k]
        return rdma(rows_block(yy, mine), rows_block(yy, mine), wb_s.at[k], wb_r.at[k], at_sib)

    def block_wait(k):
        yy = (y, down, up, opposite)[k]
        return rdma(rows_block(yy, other), rows_block(yy, other), wb_s.at[k], wb_r.at[k], at_sib)

    def z_order(i):
        return 1 + i // 2 + (i % 2) * (NZ - 2 - 2 * (i // 2))

    def g_pair(i):
        return rdma(g_send.at[i], g_recv.at[i], gs_s.at[i], gs_r.at[i], at_sib)

    def g_y(i):
        return rdma(gy_send.at[i], gy_recv.at[i], gy_s.at[i], gy_r.at[i], at_y((y + 1 + i // OWN_HEADS) % NY))

    def g_z(d):
        zz = (z + d) % NZ
        rows = gz_send.at[pl.ds(pl.multiple_of(SLAB * zz, 16), SLAB)]
        return rdma(rows, gz_recv.at[d - 1], gz_s.at[d - 1], gz_r.at[d - 1], at_z(zz))

    def g_x(d):
        xx = (x + d) % NX
        return rdma(gx_send.at[xx], gx_recv.at[d - 1], gx_s.at[d - 1], gx_r.at[d - 1], at_x(xx))

    g_c = rdma(gc_send.at[1 - c], gc_recv, gc_s, gc_r, at_sib)

    def d_pair(i):
        return rdma(d_sib.at[i], d_sib_r.at[i], ds_s.at[i], ds_r.at[i], at_sib)

    def d_far(i):
        return rdma(d_x.at[i], d_x_r.at[i], dx_s.at[i], dx_r.at[i], at_far)

    def each(count, step):
        def body(i, carry):
            step(i)
            return carry

        lax.fori_loop(0, count, body, 0)

    w_send[...] = jnp.zeros_like(w_send)
    w_send[0:DEV_ROWS] = w_own[:, other].astype(F32)
    pair_copy.start()

    def start_kv(i):
        kv_far(i).start()
        kv_sib(i).start()

    each(AHEAD, start_kv)
    q_copy.start()
    each(HEADS, lambda i: kv_own(i).start())

    def base_of(s):
        g = span[0, s]
        return s - jnp.where(g == 1, 0, jnp.where(g == 2, s % 2, s % 4))

    my_base = base_of(me)
    place = lax.broadcasted_iota(jnp.int32, (8, TOK), 1)
    for r, s in enumerate((me, sib, far, cross)):
        base = base_of(s)
        live = jnp.where(base == my_base, clip[0, s] - (s - base) * TOK, 0)
        bias_s[:, r * TOK : (r + 1) * TOK] = jnp.where(place < live, 0.0, FLOOR)

    pair_wait.wait_recv()
    w_tmp[...] = jnp.zeros_like(w_tmp)
    own_rows = w_own[:, mine].astype(F32)
    their_rows = jnp.where(c == 0, w_pair[1, 0:DEV_ROWS], w_pair[0, 0:DEV_ROWS])
    w_tmp[0:DEV_ROWS] = jnp.where(c == 0, own_rows, their_rows)
    w_tmp[DEV_ROWS:CHIP_ROWS] = jnp.where(c == 0, their_rows, own_rows)
    w_x[x] = w_tmp[...].astype(BF16)
    for d in range(1, NX):
        x_copy(d).start()
    for d in range(1, NX):
        x_wait(d).wait_recv()
    for k in range(NX):
        w_slab[k * CHIP_ROWS : (k + 1) * CHIP_ROWS] = w_x[k].astype(F32)[0:CHIP_ROWS]
    slab(y, z)[...] = w_slab[...].astype(BF16)
    for i in range(NZ - 1):
        z_copy(z_order(i)).start()
    y_copy(0, 0).start()
    y_copy(0, 1).start()

    q_copy.wait()
    each(HEADS, lambda i: kv_own(i).wait())

    def scores_of(i):
        keys = kv[i, :, :, 0:DIM].reshape(4 * TOK, DIM)
        raw = mm(q_s[head(i)], keys, NT)
        return raw * (SCALE * LOG2E) + bias_s[0:1, :]

    def o_columns(i):
        return pl.ds(pl.multiple_of(head(i) * DIM, DIM), DIM)

    def pair_sum(i):
        g_pair(i).wait_recv()
        total = g_tmp[i % 2] + g_recv[i].astype(F32)

        @pl.when(i < HEADS - OWN_HEADS)
        def _():
            k = jnp.minimum(i, HEADS - OWN_HEADS - 1)
            gy_send[k] = total.astype(BF16)
            g_y(k).start()

        @pl.when(i >= HEADS - OWN_HEADS)
        def _():
            g_acc[jnp.maximum(i - (HEADS - OWN_HEADS), 0)] = total

    def forward(i):
        @pl.when(i + AHEAD < HEADS)
        def _():
            start_kv(jnp.minimum(i + AHEAD, HEADS - 1))

        kv_far(i).wait_recv()
        kv_relay(i).start()

        @pl.when(i < NZ - 1)
        def _():
            d = z_order(jnp.minimum(i, NZ - 2))
            z_wait(d).wait_recv()
            y_copy(d, 0).start()
            y_copy(d, 1).start()

        @pl.when((i >= 1) & (i <= NZ))
        def _():
            d = jnp.where(i <= 1, 0, z_order(jnp.clip(i - 2, 0, NZ - 2)))
            y_wait(d, 0).wait_recv()
            y_wait(d, 1).wait_recv()
            y_relay(d).start()

        @pl.when(i == NZ - 1)
        def _():
            block_copy(0).start()

        @pl.when(i == NZ + 1)
        def _():
            block_copy(1).start()
            block_copy(2).start()

        @pl.when(i == NZ + 2)
        def _():
            each(NZ, lambda d: y_relay_wait(d).wait_recv())
            block_copy(3).start()

        @pl.when(i >= 1)
        def _():
            pair_sum(jnp.maximum(i - 1, 0))

        kv_sib(i).wait_recv()
        kv_relay(i).wait_recv()
        scores = scores_of(i)
        top = jnp.max(scores, axis=1, keepdims=True)
        weights = jnp.exp2(scores - top)
        total = jnp.sum(weights, axis=1, keepdims=True)
        lse_s[i] = top + jnp.log2(total)
        probs = (weights * (1.0 / total)).astype(BF16)
        values = kv[i, :, :, DIM:].reshape(4 * TOK, DIM)
        attended = mm(probs, values, NN).astype(BF16)
        o_s[:, o_columns(i)] = attended
        g_send[i] = mm(attended, gp[0, :, other], TN).astype(BF16)
        g_pair(i).start()
        g_tmp[i % 2] = mm(attended, gp[0, :, mine], TN)

    each(HEADS, forward)
    pair_sum(HEADS - 1)
    for k in range(4):
        block_wait(k).wait_recv()

    def far_send(i):
        d_pair(i).wait_recv()
        d_x[i] = (d_rs[i % 2] + d_sib_r[i, 1].astype(F32)).astype(BF16)
        d_far(i).start()

    def backward(i):
        @pl.when(i >= 1)
        def _():
            far_send(jnp.maximum(i - 1, 0))

        @pl.when(i == 2)
        def _():
            each(HEADS - OWN_HEADS, lambda k: g_y(k).wait_recv())
            for k in range(OWN_HEADS):
                total = g_acc[k]
                for source in range(NY - 1):
                    total = total + gy_recv[source * OWN_HEADS + k].astype(F32)
                g_acc[k] = total
                gz_send[k * DIM : (k + 1) * DIM] = total.astype(BF16)
            for d in range(1, NZ):
                g_z(d).start()

        h = head(i)
        w_head = w_all[pl.ds(pl.multiple_of(h * DIM, DIM), DIM), :]
        grad_att = mm(gp[0], w_head, NT).astype(BF16)
        delta = jnp.sum(grad_att.astype(F32) * o_s[:, o_columns(i)].astype(F32), axis=1, keepdims=True)
        probs = jnp.exp2(scores_of(i) - lse_s[i])
        values = kv[i, :, :, DIM:].reshape(4 * TOK, DIM)
        dprobs = mm(grad_att, values, NT)
        dscores = (probs * (dprobs - delta)).astype(BF16)
        probs_b = probs.astype(BF16)
        keys = kv[i, :, :, 0:DIM].reshape(4 * TOK, DIM)
        grad_o[0, h, :, 0:DIM] = (mm(dscores, keys, NN) * SCALE).astype(BF16)
        dk = mm(dscores, q_s[h], TN) * SCALE
        dv = mm(probs_b, grad_att, TN)
        d_own[i, :, 0:DIM] = dk[0:TOK]
        d_own[i, :, DIM:] = dv[0:TOK]
        d_sib[i, 0, :, 0:DIM] = dk[TOK : 2 * TOK].astype(BF16)
        d_sib[i, 0, :, DIM:] = dv[TOK : 2 * TOK].astype(BF16)
        d_sib[i, 1, :, 0:DIM] = dk[3 * TOK :].astype(BF16)
        d_sib[i, 1, :, DIM:] = dv[3 * TOK :].astype(BF16)
        d_pair(i).start()
        d_rs[i % 2, :, 0:DIM] = dk[2 * TOK : 3 * TOK]
        d_rs[i % 2, :, DIM:] = dv[2 * TOK : 3 * TOK]

    each(HEADS, backward)
    far_send(HEADS - 1)

    def project(k):
        columns = pl.ds(pl.multiple_of(k * TOK, TOK), TOK)
        proj_o[0, :, columns] = mm(o_s[...], w_all[:, columns], NN).astype(BF16)

    each(WIDTH // TOK, project)

    def finish(i):
        d_far(i).wait_recv()
        total = d_own[i] + d_sib_r[i, 0].astype(F32) + d_x_r[i].astype(F32)
        grad_o[0, head(i), :, DIM:] = total.astype(BF16)

    each(3, finish)

    for d in range(1, NZ):
        g_z(d).wait_recv()
    acc = g_acc.reshape(BLOCK, HALF)
    total = acc[pl.ds(pl.multiple_of(SLAB * z, 8), SLAB)]
    for d in range(1, NZ):
        total = total + gz_recv[d - 1].astype(F32)
    gx_in[...] = total
    for k in range(NX):
        gx_send[k] = jnp.zeros_like(gx_send[k])
        gx_send[k, 0:CHIP_ROWS] = gx_in[k * CHIP_ROWS : (k + 1) * CHIP_ROWS]
    for d in range(1, NX):
        g_x(d).start()

    each(3, lambda i: finish(i + 3))

    for d in range(1, NX):
        g_x(d).wait_recv()
    total = gx_send[x]
    for d in range(1, NX):
        total = total + gx_recv[d - 1]
    for k in range(2):
        gc_send[k] = jnp.zeros_like(gc_send[k])
        gc_send[k, 0:DEV_ROWS] = total[k * DEV_ROWS : (k + 1) * DEV_ROWS]
    g_c.start()

    each(HEADS - 6, lambda i: finish(i + 6))

    g_c.wait_recv()
    gw_o[:, mine] = gc_send[c, 0:DEV_ROWS]
    gw_o[:, other] = gc_recv[0:DEV_ROWS]

    def sent(i):
        kv_far(i).wait_send()
        kv_sib(i).wait_send()
        kv_relay(i).wait_send()
        g_pair(i).wait_send()
        d_pair(i).wait_send()
        d_far(i).wait_send()

    each(HEADS, sent)
    each(HEADS - OWN_HEADS, lambda i: g_y(i).wait_send())
    pair_copy.wait_send()
    g_c.wait_send()
    for d in range(1, NX):
        x_copy(d).wait_send()
        g_x(d).wait_send()
    for d in range(1, NZ):
        z_copy(d).wait_send()
        g_z(d).wait_send()

    def sent_y(d):
        y_copy(d, 0).wait_send()
        y_copy(d, 1).wait_send()
        y_relay(d).wait_send()

    each(NZ, sent_y)
    for k in range(4):
        block_copy(k).wait_send()


def local(qkv, out_weight, grad_projected, group_span, clip_length):
    vmem = functools.partial(pl.BlockSpec, memory_space=pltpu.VMEM)
    smem = functools.partial(pl.BlockSpec, memory_space=pltpu.SMEM)
    sem = pltpu.SemaphoreType.DMA
    scratch = [
        pltpu.VMEM((HEADS, TOK, DIM), BF16),
        pltpu.VMEM((HEADS, 4, TOK, 2 * DIM), BF16),
        pltpu.VMEM((8, 4 * TOK), F32),
        pltpu.VMEM((WIDTH, WIDTH), BF16),
        pltpu.VMEM((TOK, WIDTH), BF16),
        pltpu.VMEM((HEADS, TOK, 1), F32),
        pltpu.VMEM((8, HALF), F32),
        pltpu.VMEM((2, 8, HALF), F32),
        pltpu.VMEM((16, HALF), F32),
        pltpu.VMEM((NX, 16, HALF), BF16),
        pltpu.VMEM((SLAB, HALF), F32),
        pltpu.VMEM((2, DIM, HALF), F32),
        pltpu.VMEM((OWN_HEADS, DIM, HALF), F32),
        pltpu.VMEM((HEADS, DIM, HALF), BF16),
        pltpu.VMEM((HEADS, DIM, HALF), BF16),
        pltpu.VMEM((HEADS - OWN_HEADS, DIM, HALF), BF16),
        pltpu.VMEM((HEADS - OWN_HEADS, DIM, HALF), BF16),
        pltpu.VMEM((BLOCK, HALF), BF16),
        pltpu.VMEM((NZ - 1, SLAB, HALF), BF16),
        pltpu.VMEM((SLAB, HALF), F32),
        pltpu.VMEM((NX, 16, HALF), F32),
        pltpu.VMEM((NX - 1, 16, HALF), F32),
        pltpu.VMEM((2, 8, HALF), F32),
        pltpu.VMEM((8, HALF), F32),
        pltpu.VMEM((HEADS, TOK, 2 * DIM), F32),
        pltpu.VMEM((2, TOK, 2 * DIM), F32),
        pltpu.VMEM((HEADS, 2, TOK, 2 * DIM), BF16),
        pltpu.VMEM((HEADS, 2, TOK, 2 * DIM), BF16),
        pltpu.VMEM((HEADS, TOK, 2 * DIM), BF16),
        pltpu.VMEM((HEADS, TOK, 2 * DIM), BF16),
        sem((1 + HEADS,)),
        sem((HEADS,)), sem((HEADS,)),
        sem((HEADS,)), sem((HEADS,)),
        sem((HEADS,)), sem((HEADS,)),
        sem, sem,
        sem((NX - 1,)), sem((NX - 1,)),
        sem((NZ - 1,)), sem((NZ - 1,)),
        sem((NZ, 2)), sem((NZ, 2)),
        sem((NZ,)), sem((NZ,)),
        sem((4,)), sem((4,)),
        sem((HEADS,)), sem((HEADS,)),
        sem((HEADS - OWN_HEADS,)), sem((HEADS - OWN_HEADS,)),
        sem((NZ - 1,)), sem((NZ - 1,)),
        sem((NX - 1,)), sem((NX - 1,)),
        sem, sem,
        sem((HEADS,)), sem((HEADS,)),
        sem((HEADS,)), sem((HEADS,)),
    ]
    return pl.pallas_call(
        kernel,
        out_shape=(
            jax.ShapeDtypeStruct((1, TOK, WIDTH), BF16),
            jax.ShapeDtypeStruct((1, HEADS, TOK, 3 * DIM), BF16),
            jax.ShapeDtypeStruct((DEV_ROWS, WIDTH), F32),
        ),
        in_specs=[pl.BlockSpec(memory_space=pl.ANY), vmem(), vmem(), smem(), smem()],
        out_specs=(vmem(), vmem(), vmem()),
        scratch_shapes=scratch,
        compiler_params=pltpu.CompilerParams(
            collective_id=0, has_side_effects=True, vmem_limit_bytes=60 * 1024 * 1024
        ),
        cost_estimate=pl.CostEstimate(flops=10**10, bytes_accessed=10**7, transcendentals=7 * 10**6),
    )(qkv, out_weight, grad_projected, group_span, clip_length)


def solution(mesh):
    in_specs = (
        P("dp", None, "seq", None),
        P(("dp", "seq"), None),
        P("dp", "seq", None),
        P("dp", None),
        P("dp", None),
    )
    out_specs = (P("dp", "seq", None), P("dp", None, "seq", None), P(("dp", "seq"), None))
    return jax.shard_map(local, mesh=mesh, in_specs=in_specs, out_specs=out_specs, check_vma=False)
```

time: 1660 us -> 134 us (0.08); the launches traced: 1640 us -> 133 us
  blocking collectives: 714 us -> 0 us
  starting transfers between devices: 499 us -> 0 us
  local copies, waits for them, and re-layouts: 225 us -> 6.01 us
  Pallas kernels: 0 us -> 127 us
  matrix products: 78.9 us -> 0 us
  other arithmetic: 55 us -> 0 us
  waiting for transfers between devices: 39.6 us -> 0 us
  between operations: 18 us -> 0.64 us
    unnamed x1 -> x0, blocking collectives: 714 us -> none
    unnamed x64 -> x0, starting transfers between devices: 490 us -> none
    pallas_call x0 -> x1, Pallas kernels: none -> 127 us  [local(): pl.pallas_call(kernel, out_shape=(jax.ShapeDtypeStruct((1, TOK, WIDTH), B...]
    unnamed x173 -> x5, local copies, waits for them, and re-layouts: 105 us -> 6.01 us
    dot_general x87 -> x0, matrix products: 78.9 us -> none  [the longest x24 21.1 us: masked_scores(): jnp.einsum('qd,kd->qk', query_piece, key_piece, preferred_element_type=jn...]
    dynamic_slice x120 -> x0, local copies, waits for them, and re-layouts: 74.2 us -> none  [the longest x108 59.2 us: rows_of(): return lax.dynamic_slice_in_dim(array, row_start, tile_rows)]
    ppermute x8 -> x0, waiting for transfers between devices: 36.8 us -> none  [swapped_2(): return lax.ppermute(block, axis, route)]
    select_n x21 -> x0, other arithmetic: 24 us -> none  [the longest x8 10 us: butterfly(): outgoing = jnp.where(upper_half, shaped[:, 0], shaped[:, 1])]
  transfers between devices with their start and end apart: 73 -> 0, of which waited for: 6 -> 0; matrix products, arithmetic and copies ran while one was open for 57% -> 0% of each run, Pallas kernels for 0% -> 0%
where the time goes in v1:
time: 134 us; the launch traced here: 133 us
  Pallas kernels  127 us (95%)
  local copies, waits for them, and re-layouts  6.01 us (4%)
    pallas_call x1, Pallas kernels, local(): pl.pallas_call(kernel, out_shape=(jax.ShapeDtypeStruct((1, TOK, WIDTH), B...  127 us
    unnamed x5, local copies, waits for them, and re-layouts  6.01 us

profile of v1, /device:TPU:1, one launch (start us, length us, event | category | flops | bytes accessed | tf_op | source)
XLA Modules:
  0.0 133.4 jit_solution(2450690352505532325)
XLA Ops:
  0.6 126.8 %shard_map.76 = (bf16[1,256,1536]{2,1,0:T(8,128)(2,1)}, bf16[1,12,256,384]{3,2,1,0:T(8,128)(2,1)}, f32[6,1536]{1,0:T(8,128)}) custom-call(bf16[1,12,256,384]{3,2,1,0:T(8,128)(2,1)} %qkv.1, bf16[6,1536]{1,0:T(8,128)(2,1)} %w_own.1, bf16[1,256,1536]{2,1,0:T(8,128)(2,1)} %gp.1, s32[1,64]{1,0:T(1,128)} %span.1, s32[1,64]{1,0:T(1,128)} %clip.1), custom_call_target="tpu_custom_call" | custom-call | flops 10000000000 | bytes 10000000 | tf_op jit(solution)/shard_map/pallas_call | solution.py:498
  127.4 2.1 %copy.11 = bf16[1,256,1536]{2,1,0:T(8,128)(2,1)} copy(bf16[1,256,1536]{2,1,0:T(8,128)(2,1)} %get-tuple-element.6) | data formatting | bytes 1572864
  129.5 0.0 copy-start
  129.5 3.3 %copy.12 = bf16[1,12,256,384]{3,2,1,0:T(8,128)(2,1)} copy(bf16[1,12,256,384]{3,2,1,0:T(8,128)(2,1)} %get-tuple-element.7) | data formatting | bytes 4718592
  132.8 0.0 copy-done
  132.8 0.6 copy.13
Async XLA Ops:
  129.5 3.3 %copy-start = (f32[6,1536]{1,0:T(8,128)S(1)}, f32[6,1536]{1,0:T(8,128)}, u32[]{:S(2)}) copy-start(f32[6,1536]{1,0:T(8,128)} %get-tuple-element.8) | copy-start | bytes 110596

commit v2 on v1

--- a/solution.py
+++ b/solution.py
@@ -12,6 +12,7 @@
 TOK = 256
 WIDTH = 1536
 HALF = WIDTH // 2
+QUARTER = HALF // 2
 NY = 4
 NZ = 8
 NX = 4
@@ -21,6 +22,12 @@
 CHIP_ROWS = 12
 DEV_ROWS = 6
 AHEAD = 4
+LAG = 9
+WEIGHT_PASS = {1: (0, 1), 2: (2, 3), 3: (4, 5), 4: (6,)}
+WEIGHT_RELAY = {1: (0,), 3: (1, 2), 4: (3, 4), 5: (5, 6), 6: (7,)}
+WEIGHT_OWN, WEIGHT_NEAR, WEIGHT_LAST = 5, 7, 12
+G_AT = (8, 10, 11)
+GZ_AT = 16
 FLOOR = -1e30
 SCALE = DIM**-0.5
 LOG2E = 1.4426950408889634
@@ -43,12 +50,12 @@
     proj_o, grad_o, gw_o,
     q_s, kv, bias_s, w_all, o_s, lse_s,
     w_send, w_pair, w_tmp, w_x, w_slab,
-    g_tmp, g_acc, g_send, g_recv, gy_send, gy_recv, gz_send, gz_recv,
+    g_own, g_acc, g_send, g_recv, gy_send, gr_recv, gy_recv, gz_send, gz_recv,
     gx_in, gx_send, gx_recv, gc_send, gc_recv,
     d_own, d_rs, d_sib, d_sib_r, d_x, d_x_r,
     loc_sem, ks_s, ks_r, kx_s, kx_r, kf_s, kf_r,
     wa_s, wa_r, wx_s, wx_r, wz_s, wz_r, wy_s, wy_r, wf_s, wf_r, wb_s, wb_r,
-    gs_s, gs_r, gy_s, gy_r, gz_s, gz_r, gx_s, gx_r, gc_s, gc_r,
+    gs_s, gs_r, gr_s, gr_r, gy_s, gy_r, gz_s, gz_r, gx_s, gx_r, gc_s, gc_r,
     ds_s, ds_r, dx_s, dx_r,
 ):
     me = lax.axis_index("seq")
@@ -81,14 +88,19 @@
     partners = [at_sib]
     partners += [at_x((x + d) % NX) for d in range(1, NX)]
     partners += [at_z((z + d) % NZ) for d in range(1, NZ)]
-    partners += [at_y((y + d) % NY) for d in range(1, NY)]
+    partners += [at_y((y + 1) % NY), at_y((y + NY - 1) % NY)]
     barrier = pltpu.get_barrier_semaphore()
     for partner in partners:
         pl.semaphore_signal(barrier, inc=1, device_id=partner, device_id_type=MESH)
     pl.semaphore_wait(barrier, len(partners))
 
     def head(i):
-        return (OWN_HEADS * (y + 1) + i) % HEADS
+        part = i // OWN_HEADS
+        owner = y + jnp.where(part == 0, 2, jnp.where(part == 1, 1, jnp.where(part == 2, 3, 0)))
+        return (OWN_HEADS * owner + i % OWN_HEADS) % HEADS
+
+    def back_order(b):
+        return OWN_HEADS * (NY - 1 - b // OWN_HEADS) + b % OWN_HEADS
 
     def kv_sib(i):
         return rdma(qkv.at[0, head(i), :, pl.ds(DIM, 2 * DIM)], kv.at[i, 1], ks_s.at[i], ks_r.at[i], at_sib)
@@ -167,8 +179,14 @@
     def g_pair(i):
         return rdma(g_send.at[i], g_recv.at[i], gs_s.at[i], gs_r.at[i], at_sib)
 
-    def g_y(i):
-        return rdma(gy_send.at[i], gy_recv.at[i], gy_s.at[i], gy_r.at[i], at_y((y + 1 + i // OWN_HEADS) % NY))
+    def g_half(k, way):
+        columns = pl.ds(way * QUARTER, QUARTER)
+        to = at_y(up if way == 0 else down)
+        return rdma(gy_send.at[k, :, columns], gr_recv.at[way, k], gr_s.at[k, way], gr_r.at[k, way], to)
+
+    def g_y(k, way):
+        to = at_y(up if way == 0 else down)
+        return rdma(gy_send.at[OWN_HEADS * (1 + way) + k], gy_recv.at[way, k], gy_s.at[k, way], gy_r.at[k, way], to)
 
     def g_z(d):
         zz = (z + d) % NZ
@@ -249,19 +267,36 @@
 
     def pair_sum(i):
         g_pair(i).wait_recv()
-        total = g_tmp[i % 2] + g_recv[i].astype(F32)
-
-        @pl.when(i < HEADS - OWN_HEADS)
-        def _():
-            k = jnp.minimum(i, HEADS - OWN_HEADS - 1)
-            gy_send[k] = total.astype(BF16)
-            g_y(k).start()
-
-        @pl.when(i >= HEADS - OWN_HEADS)
-        def _():
-            g_acc[jnp.maximum(i - (HEADS - OWN_HEADS), 0)] = total
-
-    def forward(i):
+        return g_own[i] + g_recv[i].astype(F32)
+
+    def g_stage(part):
+        def opposite_head(k):
+            gy_send[k] = pair_sum(k).astype(BF16)
+            g_half(k, 0).start()
+            g_half(k, 1).start()
+
+        def next_head(way, k):
+            i = OWN_HEADS * (1 + way) + k
+            total = pair_sum(i)
+            g_half(k, way).wait_recv()
+            here = slice(way * QUARTER, (way + 1) * QUARTER)
+            there = slice((1 - way) * QUARTER, (2 - way) * QUARTER)
+            gy_send[i, :, there] = total[:, there].astype(BF16)
+            gy_send[i, :, here] = (total[:, here] + gr_recv[way, k].astype(F32)).astype(BF16)
+            g_y(k, way).start()
+
+        def own_head(k):
+            g_acc[k] = pair_sum(3 * OWN_HEADS + k)
+
+        steps = (
+            opposite_head,
+            functools.partial(next_head, 0),
+            functools.partial(next_head, 1),
+            own_head,
+        )
+        each(OWN_HEADS, steps[part])
+
+    def arrive(i):
         @pl.when(i + AHEAD < HEADS)
         def _():
             start_kv(jnp.minimum(i + AHEAD, HEADS - 1))
@@ -269,38 +304,7 @@
         kv_far(i).wait_recv()
         kv_relay(i).start()
 
-        @pl.when(i < NZ - 1)
-        def _():
-            d = z_order(jnp.minimum(i, NZ - 2))
-            z_wait(d).wait_recv()
-            y_copy(d, 0).start()
-            y_copy(d, 1).start()
-
-        @pl.when((i >= 1) & (i <= NZ))
-        def _():
-            d = jnp.where(i <= 1, 0, z_order(jnp.clip(i - 2, 0, NZ - 2)))
-            y_wait(d, 0).wait_recv()
-            y_wait(d, 1).wait_recv()
-            y_relay(d).start()
-
-        @pl.when(i == NZ - 1)
-        def _():
-            block_copy(0).start()
-
-        @pl.when(i == NZ + 1)
-        def _():
-            block_copy(1).start()
-            block_copy(2).start()
-
-        @pl.when(i == NZ + 2)
-        def _():
-            each(NZ, lambda d: y_relay_wait(d).wait_recv())
-            block_copy(3).start()
-
-        @pl.when(i >= 1)
-        def _():
-            pair_sum(jnp.maximum(i - 1, 0))
-
+    def forward(i):
         kv_sib(i).wait_recv()
         kv_relay(i).wait_recv()
         scores = scores_of(i)
@@ -314,34 +318,19 @@
         o_s[:, o_columns(i)] = attended
         g_send[i] = mm(attended, gp[0, :, other], TN).astype(BF16)
         g_pair(i).start()
-        g_tmp[i % 2] = mm(attended, gp[0, :, mine], TN)
-
-    each(HEADS, forward)
-    pair_sum(HEADS - 1)
-    for k in range(4):
-        block_wait(k).wait_recv()
+        g_own[i] = mm(attended, gp[0, :, mine], TN)
 
     def far_send(i):
         d_pair(i).wait_recv()
         d_x[i] = (d_rs[i % 2] + d_sib_r[i, 1].astype(F32)).astype(BF16)
         d_far(i).start()
 
-    def backward(i):
-        @pl.when(i >= 1)
+    def backward(b):
+        i = back_order(b)
+
+        @pl.when(b >= 1)
         def _():
-            far_send(jnp.maximum(i - 1, 0))
-
-        @pl.when(i == 2)
-        def _():
-            each(HEADS - OWN_HEADS, lambda k: g_y(k).wait_recv())
-            for k in range(OWN_HEADS):
-                total = g_acc[k]
-                for source in range(NY - 1):
-                    total = total + gy_recv[source * OWN_HEADS + k].astype(F32)
-                g_acc[k] = total
-                gz_send[k * DIM : (k + 1) * DIM] = total.astype(BF16)
-            for d in range(1, NZ):
-                g_z(d).start()
+            far_send(jnp.maximum(b - 1, 0))
 
         h = head(i)
         w_head = w_all[pl.ds(pl.multiple_of(h * DIM, DIM), DIM), :]
@@ -356,17 +345,90 @@
         grad_o[0, h, :, 0:DIM] = (mm(dscores, keys, NN) * SCALE).astype(BF16)
         dk = mm(dscores, q_s[h], TN) * SCALE
         dv = mm(probs_b, grad_att, TN)
-        d_own[i, :, 0:DIM] = dk[0:TOK]
-        d_own[i, :, DIM:] = dv[0:TOK]
-        d_sib[i, 0, :, 0:DIM] = dk[TOK : 2 * TOK].astype(BF16)
-        d_sib[i, 0, :, DIM:] = dv[TOK : 2 * TOK].astype(BF16)
-        d_sib[i, 1, :, 0:DIM] = dk[3 * TOK :].astype(BF16)
-        d_sib[i, 1, :, DIM:] = dv[3 * TOK :].astype(BF16)
-        d_pair(i).start()
-        d_rs[i % 2, :, 0:DIM] = dk[2 * TOK : 3 * TOK]
-        d_rs[i % 2, :, DIM:] = dv[2 * TOK : 3 * TOK]
-
-    each(HEADS, backward)
+        d_own[b, :, 0:DIM] = dk[0:TOK]
+        d_own[b, :, DIM:] = dv[0:TOK]
+        d_sib[b, 0, :, 0:DIM] = dk[TOK : 2 * TOK].astype(BF16)
+        d_sib[b, 0, :, DIM:] = dv[TOK : 2 * TOK].astype(BF16)
+        d_sib[b, 1, :, 0:DIM] = dk[3 * TOK :].astype(BF16)
+        d_sib[b, 1, :, DIM:] = dv[3 * TOK :].astype(BF16)
+        d_pair(b).start()
+        d_rs[b % 2, :, 0:DIM] = dk[2 * TOK : 3 * TOK]
+        d_rs[b % 2, :, DIM:] = dv[2 * TOK : 3 * TOK]
+
+    def pass_slab(n):
+        d = z_order(n)
+        z_wait(d).wait_recv()
+        y_copy(d, 0).start()
+        y_copy(d, 1).start()
+
+    def relay_slab(d):
+        y_wait(d, 0).wait_recv()
+        y_wait(d, 1).wait_recv()
+        y_relay(d).start()
+
+    def weight_step(t):
+        for n in WEIGHT_PASS.get(t, ()):
+            pass_slab(n)
+        for n in WEIGHT_RELAY.get(t, ()):
+            relay_slab(0 if n == 0 else z_order(n - 1))
+        if t == WEIGHT_OWN:
+            block_copy(0).start()
+        if t == WEIGHT_NEAR:
+            block_copy(1).start()
+            block_copy(2).start()
+        if t == WEIGHT_LAST:
+            for d in range(NZ):
+                y_relay_wait(d).wait_recv()
+            block_copy(3).start()
+
+    def own_sum():
+        g_stage(3)
+        for k in range(OWN_HEADS):
+            g_y(k, 0).wait_recv()
+            g_y(k, 1).wait_recv()
+            total = g_acc[k] + gy_recv[0, k].astype(F32) + gy_recv[1, k].astype(F32)
+            g_acc[k] = total
+            gz_send[k * DIM : (k + 1) * DIM] = total.astype(BF16)
+        for d in range(1, NZ):
+            g_z(d).start()
+
+    def step(t):
+        @pl.when(t < HEADS)
+        def _():
+            i = jnp.minimum(t, HEADS - 1)
+            arrive(i)
+
+        for at in range(WEIGHT_LAST + 1):
+
+            @pl.when(t == at)
+            def _(at=at):
+                weight_step(at)
+
+        for part, at in enumerate(G_AT):
+
+            @pl.when(t == at)
+            def _(part=part):
+                g_stage(part)
+
+        @pl.when(t == GZ_AT)
+        def _():
+            own_sum()
+
+        for k in range(4):
+
+            @pl.when(t == LAG + OWN_HEADS * k)
+            def _(k=k):
+                block_wait(k).wait_recv()
+
+        @pl.when(t < HEADS)
+        def _():
+            forward(jnp.minimum(t, HEADS - 1))
+
+        @pl.when(t >= LAG)
+        def _():
+            backward(jnp.maximum(t - LAG, 0))
+
+    each(HEADS + LAG, step)
     far_send(HEADS - 1)
 
     def project(k):
@@ -378,7 +440,7 @@
     def finish(i):
         d_far(i).wait_recv()
         total = d_own[i] + d_sib_r[i, 0].astype(F32) + d_x_r[i].astype(F32)
-        grad_o[0, head(i), :, DIM:] = total.astype(BF16)
+        grad_o[0, head(back_order(i)), :, DIM:] = total.astype(BF16)
 
     each(3, finish)
 
@@ -422,7 +484,13 @@
         d_far(i).wait_send()
 
     each(HEADS, sent)
-    each(HEADS - OWN_HEADS, lambda i: g_y(i).wait_send())
+
+    def sent_g(k):
+        for way in range(2):
+            g_half(k, way).wait_send()
+            g_y(k, way).wait_send()
+
+    each(OWN_HEADS, sent_g)
     pair_copy.wait_send()
     g_c.wait_send()
     for d in range(1, NX):
@@ -458,12 +526,13 @@
         pltpu.VMEM((16, HALF), F32),
         pltpu.VMEM((NX, 16, HALF), BF16),
         pltpu.VMEM((SLAB, HALF), F32),
-        pltpu.VMEM((2, DIM, HALF), F32),
+        pltpu.VMEM((HEADS, DIM, HALF), F32),
         pltpu.VMEM((OWN_HEADS, DIM, HALF), F32),
         pltpu.VMEM((HEADS, DIM, HALF), BF16),
         pltpu.VMEM((HEADS, DIM, HALF), BF16),
         pltpu.VMEM((HEADS - OWN_HEADS, DIM, HALF), BF16),
-        pltpu.VMEM((HEADS - OWN_HEADS, DIM, HALF), BF16),
+        pltpu.VMEM((2, OWN_HEADS, DIM, QUARTER), BF16),
+        pltpu.VMEM((2, OWN_HEADS, DIM, HALF), BF16),
         pltpu.VMEM((BLOCK, HALF), BF16),
         pltpu.VMEM((NZ - 1, SLAB, HALF), BF16),
         pltpu.VMEM((SLAB, HALF), F32),
@@ -488,7 +557,8 @@
         sem((NZ,)), sem((NZ,)),
         sem((4,)), sem((4,)),
         sem((HEADS,)), sem((HEADS,)),
-        sem((HEADS - OWN_HEADS,)), sem((HEADS - OWN_HEADS,)),
+        sem((OWN_HEADS, 2)), sem((OWN_HEADS, 2)),
+        sem((OWN_HEADS, 2)), sem((OWN_HEADS, 2)),
         sem((NZ - 1,)), sem((NZ - 1,)),
         sem((NX - 1,)), sem((NX - 1,)),
         sem, sem,

time: 134 us -> 114 us (0.85)
  Pallas kernels: 127 us -> 108 us
    pallas_call x1, Pallas kernels: 127 us -> 108 us  [local(): pl.pallas_call(kernel, out_shape=(jax.ShapeDtypeStruct((1, TOK, WIDTH), B...]
where the time goes in v2:
time: 114 us
  Pallas kernels  108 us (95%)
  local copies, waits for them, and re-layouts  6.01 us (5%)
    pallas_call x1, Pallas kernels, local(): pl.pallas_call(kernel, out_shape=(jax.ShapeDtypeStruct((1, TOK, WIDTH), B...  108 us
    unnamed x5, local copies, waits for them, and re-layouts  6.01 us

profile of v2, /device:TPU:1, one launch (start us, length us, event | category | flops | bytes accessed | tf_op | source)
XLA Modules:
  0.0 114.3 jit_solution(8085009721136004130)
XLA Ops:
  0.6 107.6 %shard_map.76 = (bf16[1,256,1536]{2,1,0:T(8,128)(2,1)}, bf16[1,12,256,384]{3,2,1,0:T(8,128)(2,1)}, f32[6,1536]{1,0:T(8,128)}) custom-call(bf16[1,12,256,384]{3,2,1,0:T(8,128)(2,1)} %qkv.1, bf16[6,1536]{1,0:T(8,128)(2,1)} %w_own.1, bf16[1,256,1536]{2,1,0:T(8,128)(2,1)} %gp.1, s32[1,64]{1,0:T(1,128)} %span.1, s32[1,64]{1,0:T(1,128)} %clip.1), custom_call_target="tpu_custom_call" | custom-call | flops 10000000000 | bytes 10000000 | tf_op jit(solution)/shard_map/pallas_call | solution.py:568
  108.3 2.1 %copy.11 = bf16[1,256,1536]{2,1,0:T(8,128)(2,1)} copy(bf16[1,256,1536]{2,1,0:T(8,128)(2,1)} %get-tuple-element.6) | data formatting | bytes 1572864
  110.3 0.0 copy-start
  110.3 3.3 %copy.12 = bf16[1,12,256,384]{3,2,1,0:T(8,128)(2,1)} copy(bf16[1,12,256,384]{3,2,1,0:T(8,128)(2,1)} %get-tuple-element.7) | data formatting | bytes 4718592
  113.7 0.0 copy-done
  113.7 0.6 copy.13
Async XLA Ops:
  110.3 3.3 %copy-start = (f32[6,1536]{1,0:T(8,128)S(1)}, f32[6,1536]{1,0:T(8,128)}, u32[]{:S(2)}) copy-start(f32[6,1536]{1,0:T(8,128)} %get-tuple-element.8) | copy-start | bytes 110596

commit v3 on v2

--- a/solution.py
+++ b/solution.py
@@ -21,11 +21,12 @@
 OWN_HEADS = HEADS // NY
 CHIP_ROWS = 12
 DEV_ROWS = 6
-AHEAD = 4
+AHEAD = 2
 LAG = 9
-WEIGHT_PASS = {1: (0, 1), 2: (2, 3), 3: (4, 5), 4: (6,)}
-WEIGHT_RELAY = {1: (0,), 3: (1, 2), 4: (3, 4), 5: (5, 6), 6: (7,)}
-WEIGHT_OWN, WEIGHT_NEAR, WEIGHT_LAST = 5, 7, 12
+WEIGHT_SEND = {0: (2, 3), 1: (4, 5), 2: (6,)}
+WEIGHT_PASS = {2: (0, 1), 3: (2, 3), 4: (4, 5), 5: (6,)}
+WEIGHT_RELAY = {2: (0,), 4: (1, 2), 5: (3, 4), 6: (5, 6), 7: (7,)}
+WEIGHT_OWN, WEIGHT_NEAR, WEIGHT_LAST = 6, 8, 13
 G_AT = (8, 10, 11)
 GZ_AT = 16
 FLOOR = -1e30
@@ -249,7 +250,7 @@
     for k in range(NX):
         w_slab[k * CHIP_ROWS : (k + 1) * CHIP_ROWS] = w_x[k].astype(F32)[0:CHIP_ROWS]
     slab(y, z)[...] = w_slab[...].astype(BF16)
-    for i in range(NZ - 1):
+    for i in range(2):
         z_copy(z_order(i)).start()
     y_copy(0, 0).start()
     y_copy(0, 1).start()
@@ -367,6 +368,8 @@
         y_relay(d).start()
 
     def weight_step(t):
+        for n in WEIGHT_SEND.get(t, ()):
+            z_copy(z_order(n)).start()
         for n in WEIGHT_PASS.get(t, ()):
             pass_slab(n)
         for n in WEIGHT_RELAY.get(t, ()):
@@ -389,8 +392,6 @@
             total = g_acc[k] + gy_recv[0, k].astype(F32) + gy_recv[1, k].astype(F32)
             g_acc[k] = total
             gz_send[k * DIM : (k + 1) * DIM] = total.astype(BF16)
-        for d in range(1, NZ):
-            g_z(d).start()
 
     def step(t):
         @pl.when(t < HEADS)
@@ -413,6 +414,13 @@
         @pl.when(t == GZ_AT)
         def _():
             own_sum()
+
+        for part in range(4):
+
+            @pl.when(t == GZ_AT + part)
+            def _(part=part):
+                for n in (2 * part, 2 * part + 1)[: NZ - 1 - 2 * part]:
+                    g_z(z_order(n)).start()
 
         for k in range(4):
 
@@ -508,6 +516,19 @@
     each(NZ, sent_y)
     for k in range(4):
         block_copy(k).wait_send()
+
+
+def hand_over(proj, grad, gw, proj_o, grad_o, gw_o, sems):
+    copies = [pltpu.make_async_copy(gw, gw_o, sems.at[0])]
+    for k in range(2):
+        rows = pl.ds(k * (TOK // 2), TOK // 2)
+        copies.append(pltpu.make_async_copy(proj.at[0, rows], proj_o.at[0, rows], sems.at[1 + k]))
+    for h in range(HEADS):
+        copies.append(pltpu.make_async_copy(grad.at[0, h], grad_o.at[0, h], sems.at[3 + h]))
+    for copy in copies:
+        copy.start()
+    for copy in copies:
+        copy.wait()
 
 
 def local(qkv, out_weight, grad_projected, group_span, clip_length):
@@ -565,7 +586,7 @@
         sem((HEADS,)), sem((HEADS,)),
         sem((HEADS,)), sem((HEADS,)),
     ]
-    return pl.pallas_call(
+    results = pl.pallas_call(
         kernel,
         out_shape=(
             jax.ShapeDtypeStruct((1, TOK, WIDTH), BF16),
@@ -580,6 +601,14 @@
         ),
         cost_estimate=pl.CostEstimate(flops=10**10, bytes_accessed=10**7, transcendentals=7 * 10**6),
     )(qkv, out_weight, grad_projected, group_span, clip_length)
+    hbm = functools.partial(pl.BlockSpec, memory_space=pl.ANY)
+    return pl.pallas_call(
+        hand_over,
+        out_shape=tuple(jax.ShapeDtypeStruct(r.shape, r.dtype) for r in results),
+        in_specs=[vmem(), vmem(), vmem()],
+        out_specs=(hbm(), hbm(), hbm()),
+        scratch_shapes=[sem((HEADS + 3,))],
+    )(*results)
 
 
 def solution(mesh):

time: 114 us -> 104 us (0.912)
  local copies, waits for them, and re-layouts: 6.01 us -> 0 us
  Pallas kernels: 108 us -> 103 us
    pallas_call x1, Pallas kernels: 108 us -> 99.4 us  [local(): pl.pallas_call(kernel, out_shape=(jax.ShapeDtypeStruct((1, TOK, WIDTH), B...]
    unnamed x5 -> x0, local copies, waits for them, and re-layouts: 6.01 us -> none
    pallas_call x0 -> x1, Pallas kernels: none -> 3.64 us  [local(): pl.pallas_call(hand_over, out_shape=tuple((jax.ShapeDtypeStruct(r.shape,...]
where the time goes in v3:
time: 104 us
  Pallas kernels  103 us (99%)
    pallas_call x1, Pallas kernels, local(): pl.pallas_call(kernel, out_shape=(jax.ShapeDtypeStruct((1, TOK, WIDTH), B...  99.4 us
    pallas_call x1, Pallas kernels, local(): pl.pallas_call(hand_over, out_shape=tuple((jax.ShapeDtypeStruct(r.shape,...  3.64 us

profile of v3, /device:TPU:1, one launch (start us, length us, event | category | flops | bytes accessed | tf_op | source)
XLA Modules:
  0.0 103.7 jit_solution(2026558878907821286)
XLA Ops:
  0.6 99.4 %shard_map.76 = (bf16[1,256,1536]{2,1,0:T(8,128)(2,1)}, bf16[1,12,256,384]{3,2,1,0:T(8,128)(2,1)}, f32[6,1536]{1,0:T(8,128)}) custom-call(bf16[1,12,256,384]{3,2,1,0:T(8,128)(2,1)} %qkv.1, bf16[6,1536]{1,0:T(8,128)(2,1)} %w_own.1, bf16[1,256,1536]{2,1,0:T(8,128)(2,1)} %gp.1, s32[1,64]{1,0:T(1,128)} %span.1, s32[1,64]{1,0:T(1,128)} %clip.1), custom_call_target="tpu_custom_call" | custom-call | flops 10000000000 | bytes 10000000 | tf_op jit(solution)/shard_map/pallas_call | solution.py:589
  100.1 3.6 %shard_map.77 = (bf16[1,256,1536]{2,1,0:T(8,128)(2,1)}, bf16[1,12,256,384]{3,2,1,0:T(8,128)(2,1)}, f32[6,1536]{1,0:T(8,128)}) custom-call(bf16[1,256,1536]{2,1,0:T(8,128)(2,1)} %get-tuple-element.6.proj, bf16[1,12,256,384]{3,2,1,0:T(8,128)(2,1)} %get-tuple-element.7.grad, f32[6,1536]{1,0:T(8,128)} %get-tuple-element.8.gw), custom_call_target="tpu_custom_call" | custom-call | tf_op jit(solution)/shard_map/pallas_call | solution.py:605

commit v4 on v3

--- a/solution.py
+++ b/solution.py
@@ -221,7 +221,7 @@
         kv_far(i).start()
         kv_sib(i).start()
 
-    each(AHEAD, start_kv)
+    start_kv(0)
     q_copy.start()
     each(HEADS, lambda i: kv_own(i).start())
 
@@ -245,6 +245,7 @@
     w_x[x] = w_tmp[...].astype(BF16)
     for d in range(1, NX):
         x_copy(d).start()
+    start_kv(1)
     for d in range(1, NX):
         x_wait(d).wait_recv()
     for k in range(NX):

time: 104 us -> 102 us (0.981)
  Pallas kernels: 103 us -> 101 us
    pallas_call x1, Pallas kernels: 99.4 us -> 97.8 us  [local(): pl.pallas_call(kernel, out_shape=(jax.ShapeDtypeStruct((1, TOK, WIDTH), B...]
where the time goes in v4:
time: 102 us
  Pallas kernels  101 us (99%)
    pallas_call x1, Pallas kernels, local(): pl.pallas_call(kernel, out_shape=(jax.ShapeDtypeStruct((1, TOK, WIDTH), B...  97.8 us
    pallas_call x1, Pallas kernels, local(): pl.pallas_call(hand_over, out_shape=tuple((jax.ShapeDtypeStruct(r.shape,...  3.64 us

profile of v4, /device:TPU:1, one launch (start us, length us, event | category | flops | bytes accessed | tf_op | source)
XLA Modules:
  0.0 102.1 jit_solution(10911016192376974028)
XLA Ops:
  0.6 97.8 %shard_map.76 = (bf16[1,256,1536]{2,1,0:T(8,128)(2,1)}, bf16[1,12,256,384]{3,2,1,0:T(8,128)(2,1)}, f32[6,1536]{1,0:T(8,128)}) custom-call(bf16[1,12,256,384]{3,2,1,0:T(8,128)(2,1)} %qkv.1, bf16[6,1536]{1,0:T(8,128)(2,1)} %w_own.1, bf16[1,256,1536]{2,1,0:T(8,128)(2,1)} %gp.1, s32[1,64]{1,0:T(1,128)} %span.1, s32[1,64]{1,0:T(1,128)} %clip.1), custom_call_target="tpu_custom_call" | custom-call | flops 10000000000 | bytes 10000000 | tf_op jit(solution)/shard_map/pallas_call | solution.py:590
  98.4 3.6 %shard_map.77 = (bf16[1,256,1536]{2,1,0:T(8,128)(2,1)}, bf16[1,12,256,384]{3,2,1,0:T(8,128)(2,1)}, f32[6,1536]{1,0:T(8,128)}) custom-call(bf16[1,256,1536]{2,1,0:T(8,128)(2,1)} %get-tuple-element.6.proj, bf16[1,12,256,384]{3,2,1,0:T(8,128)(2,1)} %get-tuple-element.7.grad, f32[6,1536]{1,0:T(8,128)} %get-tuple-element.8.gw), custom_call_target="tpu_custom_call" | custom-call | tf_op jit(solution)/shard_map/pallas_call | solution.py:606

commit v5 on v4

--- a/solution.py
+++ b/solution.py
@@ -27,8 +27,8 @@
 WEIGHT_PASS = {2: (0, 1), 3: (2, 3), 4: (4, 5), 5: (6,)}
 WEIGHT_RELAY = {2: (0,), 4: (1, 2), 5: (3, 4), 6: (5, 6), 7: (7,)}
 WEIGHT_OWN, WEIGHT_NEAR, WEIGHT_LAST = 6, 8, 13
-G_AT = (8, 10, 11)
-GZ_AT = 16
+G_AT = (7, 10, 11)
+GZ_AT = 17
 FLOOR = -1e30
 SCALE = DIM**-0.5
 LOG2E = 1.4426950408889634

time: 102 us -> 102 us (level)
  no operation moved by 1% of the time
where the time goes in v5:
time: 102 us
  Pallas kernels  101 us (99%)
    pallas_call x1, Pallas kernels, local(): pl.pallas_call(kernel, out_shape=(jax.ShapeDtypeStruct((1, TOK, WIDTH), B...  97.5 us
    pallas_call x1, Pallas kernels, local(): pl.pallas_call(hand_over, out_shape=tuple((jax.ShapeDtypeStruct(r.shape,...  3.64 us

profile of v5, /device:TPU:1, one launch (start us, length us, event | category | flops | bytes accessed | tf_op | source)
XLA Modules:
  0.0 101.8 jit_solution(16667663466879280834)
XLA Ops:
  0.6 97.5 %shard_map.76 = (bf16[1,256,1536]{2,1,0:T(8,128)(2,1)}, bf16[1,12,256,384]{3,2,1,0:T(8,128)(2,1)}, f32[6,1536]{1,0:T(8,128)}) custom-call(bf16[1,12,256,384]{3,2,1,0:T(8,128)(2,1)} %qkv.1, bf16[6,1536]{1,0:T(8,128)(2,1)} %w_own.1, bf16[1,256,1536]{2,1,0:T(8,128)(2,1)} %gp.1, s32[1,64]{1,0:T(1,128)} %span.1, s32[1,64]{1,0:T(1,128)} %clip.1), custom_call_target="tpu_custom_call" | custom-call | flops 10000000000 | bytes 10000000 | tf_op jit(solution)/shard_map/pallas_call | solution.py:590
  98.1 3.6 %shard_map.77 = (bf16[1,256,1536]{2,1,0:T(8,128)(2,1)}, bf16[1,12,256,384]{3,2,1,0:T(8,128)(2,1)}, f32[6,1536]{1,0:T(8,128)}) custom-call(bf16[1,256,1536]{2,1,0:T(8,128)(2,1)} %get-tuple-element.6.proj, bf16[1,12,256,384]{3,2,1,0:T(8,128)(2,1)} %get-tuple-element.7.grad, f32[6,1536]{1,0:T(8,128)} %get-tuple-element.8.gw), custom_call_target="tpu_custom_call" | custom-call | tf_op jit(solution)/shard_map/pallas_call | solution.py:606
